TPU v7x, 128 devices: a whole 4x4x4 slice. The times are simulated.
128 devices in a mesh: grp: 2 (over z_hi), ch: 64 (over y, x, z_lo, core).
Axes of the slice: x: 4, y: 4, z: 4 (z_hi: 2, z_lo: 2; z = z_hi * 2 + z_lo), core: 2. Of those that a mesh axis runs over, the one named last changes fastest.
Arguments:
- hidden: bfloat16 [65536, 768], P(('grp', 'ch')), may hold values from -6 to 6
- cotangent: bfloat16 [65536, 768], P(('grp', 'ch')), may hold values from -6 to 6
- lengths: int32 [128], replicated, may hold values from 259 to 512, as said below
- split_at: int32 [128], replicated, may hold values from 1 to 510, as said below
- seg_table: float32 [2, 768], replicated, may hold values from -3 to 3
- w_query: bfloat16 [2, 768, 384], replicated, may hold values from -0.21875 to 0.21875
- b_query: float32 [2, 384], replicated, may hold values from -3 to 3
- w_key: bfloat16 [2, 768, 384], replicated, may hold values from -0.21875 to 0.21875
- w_value: bfloat16 [2, 768, 384], replicated, may hold values from -0.21875 to 0.21875
- b_value: float32 [2, 384], replicated, may hold values from -3 to 3
- w_depth: bfloat16 [2, 9, 768], replicated, may hold values from -2 to 2
- w_point: bfloat16 [2, 768, 384], replicated, may hold values from -0.21875 to 0.21875
- b_keyconv: float32 [2, 384], replicated, may hold values from -3 to 3
- w_kernel: bfloat16 [2, 384, 54], replicated, may hold values from -0.3125 to 0.3125
- b_kernel: float32 [2, 54], replicated, may hold values from -4 to 4
- w_conv: bfloat16 [2, 768, 384], replicated, may hold values from -0.21875 to 0.21875
- b_conv: float32 [2, 384], replicated, may hold values from -3 to 3
- w_out: bfloat16 [2, 768, 768], replicated, may hold values from -0.875 to 0.875
- b_out: float32 [2, 768], replicated, may hold values from -2 to 2
- first_gain: float32 [2, 768], replicated, may hold values from 0.25 to 1.75
- first_shift: float32 [2, 768], replicated, may hold values from -2 to 2
- w_up: bfloat16 [2, 2, 384, 1536], P(None, 'grp', None, 'ch'), may hold values from -0.3125 to 0.3125
- b_up: bfloat16 [2, 2, 1536], P(None, 'grp', 'ch'), may hold values from -3 to 3
- down_weight: bfloat16 [2, 2, 1536, 384], P(None, 'grp', 'ch'), may hold values from -0.15625 to 0.15625
- b_down: float32 [2, 768], replicated, may hold values from -2 to 2
- second_gain: float32 [2, 768], replicated, may hold values from 0.25 to 1.75
- second_shift: float32 [2, 768], replicated, may hold values from -2 to 2
Outputs:
- output: float32 [65536, 768], P(('grp', 'ch'))
- input_grad: float32 [65536, 768], P(('grp', 'ch'))
- grad_seg_table: float32 [2, 768], replicated
- grad_w_query: float32 [2, 768, 384], replicated
- grad_b_query: float32 [2, 384], replicated
- grad_w_key: float32 [2, 768, 384], replicated
- grad_w_value: float32 [2, 768, 384], replicated
- grad_b_value: float32 [2, 384], replicated
- grad_w_depth: float32 [2, 9, 768], replicated
- grad_w_point: float32 [2, 768, 384], replicated
- grad_b_keyconv: float32 [2, 384], replicated
- grad_w_kernel: float32 [2, 384, 54], replicated
- grad_b_kernel: float32 [2, 54], replicated
- grad_w_conv: float32 [2, 768, 384], replicated
- grad_b_conv: float32 [2, 384], replicated
- grad_w_out: float32 [2, 768, 768], replicated
- grad_b_out: float32 [2, 768], replicated
- grad_first_gain: float32 [2, 768], replicated
- grad_first_shift: float32 [2, 768], replicated
- grad_w_up: float32 [2, 2, 384, 1536], P(None, 'grp', None, 'ch')
- grad_b_up: float32 [2, 2, 1536], P(None, 'grp', 'ch')
- grad_w_down: float32 [2, 2, 1536, 384], P(None, 'grp', 'ch')
- grad_b_down: float32 [2, 768], replicated
- grad_second_gain: float32 [2, 768], replicated
- grad_second_shift: float32 [2, 768], replicated
Inputs may be any that keep to these rules, and one draw needn't show every extreme that they name: `lengths`: one row in every draw has exactly 512 live positions and another exactly 259. `split_at`: lies between 1 and the row's length minus 2.
All inputs are finite; a program needn't handle non-finite values.
Results may differ from a plain program's by a relative error of at most 0.025.
Values may be sent and summed in bfloat16 or wider, within the bound.
A program may use at most 320 MiB of HBM per device.

v0:
```python
import jax
import jax.numpy as jnp
from jax import lax
from jax.sharding import Mesh
from jax.sharding import PartitionSpec as P

HEADS = 6
HEAD = 64
KERNEL = 9
LAYERS = 2
LEN = 512
CH = ("ch_0", "ch_1", "ch_2", "ch_3")
GRP_CH = ("grp", "ch_0", "ch_1", "ch_2", "ch_3")


EPSILON = 1e-06
SCORE_SCALE = 0.125
MASK_VALUE = -1000000000.0


def gather_turned(arrays, axis, dims):
    turned = [jnp.moveaxis(a, dim, 0) for a, dim in zip(arrays, dims)]
    both = jnp.concatenate([t.reshape(len(t), -1) for t in turned], axis=1)
    whole, at, finished = (lax.all_gather(both, axis, axis=0, tiled=True), 0, [])
    for t, dim in zip(turned, dims):
        piece = whole[:, at : at + t[0].size].reshape(-1, *t.shape[1:])
        finished.append(jnp.moveaxis(piece, 0, dim))
        at += t[0].size
    return tuple(finished)


def cut_along(x, dim, length):
    shape = x.shape
    tiles = x.reshape(*shape[:dim], length, shape[dim] // length, *shape[dim + 1 :])
    return jnp.moveaxis(tiles, dim, 0)


def summed_on_arrival(x, axis, dim):
    tiles = cut_along(x, dim, lax.axis_size(axis))
    arrived = lax.all_to_all(tiles, axis, split_axis=0, concat_axis=0, tiled=True)
    return arrived.sum(axis=0)


def summed_rows(x, axes, dim):
    far, near = axes
    tiles = cut_along(x, dim, lax.axis_size(far))
    nearer = summed_on_arrival(tiles, near, dim + 1)
    arrived = lax.all_to_all(nearer, far, split_axis=0, concat_axis=0, tiled=True)
    return arrived.sum(axis=0)


def side_by_side(arrays, axis, dim, along):
    columns = [a.reshape(*a.shape[:along], -1) for a in arrays]
    both = jnp.concatenate(columns, axis=along)
    whole, at, finished = (summed_rows(both, axis, dim), 0, [])
    for a, column in zip(arrays, columns):
        piece = whole[..., at : at + column.shape[along]]
        finished.append(piece.reshape(*piece.shape[:along], *a.shape[along:]))
        at += column.shape[along]
    return tuple(finished)


def norm_rows(residual, gains, offset):
    center = residual - jnp.mean(residual, axis=-1, keepdims=True)
    spread = jnp.mean(center * center, axis=-1, keepdims=True)
    return center * lax.rsqrt(spread + EPSILON) * gains + offset


def product(first_op, second_op):
    return jnp.dot(first_op, second_op, preferred_element_type=jnp.float32)


def product_t(first_op, second_op):
    return lax.dot_general(
        first_op, second_op, (((1,), (1,)), ((), ())), preferred_element_type=jnp.float32
    )


def inner_rows(first_op, second_op):
    return lax.dot_general(
        first_op, second_op, (((0,), (0,)), ((), ())), preferred_element_type=jnp.float32
    )


def exact_gelu(inputs):
    return jax.nn.gelu(inputs, approximate=False)


def column_sum(inputs):
    return jnp.sum(inputs.astype(jnp.float32), axis=0)


def attend_forward(operands):
    query_low, key_heads, value_heads, key_valid = operands
    scores = (
        jnp.einsum("qhd,khd->hqk", query_low, key_heads, preferred_element_type=jnp.float32)
        * SCORE_SCALE
    )
    scores = jnp.where(key_valid[None, None, :], scores, MASK_VALUE)
    peak = jnp.max(scores, axis=-1, keepdims=True)
    log_total = peak + jnp.log(jnp.sum(jnp.exp(scores - peak), axis=-1, keepdims=True))
    probs_low = jnp.exp(scores - log_total).astype(jnp.bfloat16)
    context = jnp.einsum("hqk,khd->qhd", probs_low, value_heads, preferred_element_type=jnp.float32)
    return (context.reshape(context.shape[0], -1), log_total)


def attend_backward(operands):
    query_low, key_heads, value_heads, d_context, log_total, key_valid = operands
    scores = (
        jnp.einsum("qhd,khd->hqk", query_low, key_heads, preferred_element_type=jnp.float32)
        * SCORE_SCALE
    )
    scores = jnp.where(key_valid[None, None, :], scores, MASK_VALUE)
    probs = jnp.exp(scores - log_total)
    d_probs = jnp.einsum("qhd,khd->hqk", d_context, value_heads, preferred_element_type=jnp.float32)
    row_dot = jnp.sum(probs * d_probs, axis=-1, keepdims=True)
    d_scores = (probs * (d_probs - row_dot)).astype(jnp.bfloat16)
    d_query_att = (
        jnp.einsum("hqk,khd->qhd", d_scores, key_heads, preferred_element_type=jnp.float32)
        * SCORE_SCALE
    )
    d_key = (
        jnp.einsum("hqk,qhd->khd", d_scores, query_low, preferred_element_type=jnp.float32)
        * SCORE_SCALE
    ).astype(jnp.bfloat16)
    d_value = jnp.einsum(
        "hqk,qhd->khd", probs.astype(jnp.bfloat16), d_context, preferred_element_type=jnp.float32
    ).astype(jnp.bfloat16)
    seq_rows = query_low.shape[0]
    return (
        d_query_att.reshape(seq_rows, -1),
        d_key.reshape(seq_rows, -1),
        d_value.reshape(seq_rows, -1),
    )


def shards(
    hidden,
    cotangent,
    lengths,
    split_at,
    seg_table,
    w_query,
    b_query,
    w_key,
    w_value,
    b_value,
    w_depth,
    w_point,
    b_keyconv,
    w_kernel,
    b_kernel,
    w_conv,
    b_conv,
    w_out,
    b_out,
    first_gain,
    first_shift,
    w_up,
    b_up,
    down_weight,
    b_down,
    second_gain,
    second_shift,
):
    num_rows = hidden.shape[0]
    model_width = hidden.shape[1]
    attend = w_query.shape[2]
    half_width = model_width // 2
    conv_reach = KERNEL // 2
    seq_count = num_rows // LEN
    block_index = lax.axis_index("grp") * lax.axis_size(CH) + lax.axis_index(CH)
    first_seq = block_index * seq_count
    my_lengths = lax.dynamic_slice_in_dim(lengths, first_seq, seq_count)
    my_splits = lax.dynamic_slice_in_dim(split_at, first_seq, seq_count)
    positions = jnp.arange(LEN, dtype=jnp.int32)
    key_valid = positions[None, :] < my_lengths[:, None]
    valid_rows = key_valid.astype(jnp.float32).reshape(num_rows, 1)
    second_seg = (positions[None, :] > my_splits[:, None]).reshape(num_rows, 1)
    start_x = (
        hidden.astype(jnp.float32) + jnp.where(second_seg, seg_table[1], seg_table[0])
    ) * valid_rows

    def rows_three(matrix):
        return matrix.reshape(seq_count, LEN, matrix.shape[-1])

    def pad_rows(matrix):
        return jnp.pad(matrix, ((0, 0), (conv_reach, conv_reach), (0, 0)))

    def heads_four(matrix):
        return matrix.reshape(seq_count, LEN, HEADS, HEAD)

    def conv_kernels(queries, key_conv, layer_number):
        mixed = key_conv * queries
        kernel_logit = (
            product(mixed.astype(jnp.bfloat16), w_kernel[layer_number]) + b_kernel[layer_number]
        )
        return (mixed, jax.nn.softmax(kernel_logit.reshape(seq_count, LEN, HEADS, KERNEL), axis=-1))

    def forward_layer(layer_input, layer_number):
        x_low = layer_input.astype(jnp.bfloat16)
        queries = product(x_low, w_query[layer_number]) + b_query[layer_number]
        key_low = product(x_low, w_key[layer_number]).astype(jnp.bfloat16)
        value_low = (product(x_low, w_value[layer_number]) + b_value[layer_number]).astype(
            jnp.bfloat16
        )
        x_pad = pad_rows(rows_three(x_low)).astype(jnp.float32)
        depth_taps = w_depth[layer_number].astype(jnp.float32)
        depth_out = sum(
            (depth_taps[tap_idx] * x_pad[:, tap_idx : tap_idx + LEN] for tap_idx in range(KERNEL))
        ).reshape(num_rows, model_width)
        depth_low = depth_out.astype(jnp.bfloat16)
        key_conv = product(depth_low, w_point[layer_number]) + b_keyconv[layer_number]
        mixed, kernels = conv_kernels(queries, key_conv, layer_number)
        conv_rows = product(x_low, w_conv[layer_number]) + b_conv[layer_number]
        conv_pad = pad_rows(rows_three(conv_rows)).reshape(
            seq_count, LEN + 2 * conv_reach, HEADS, HEAD
        )
        conv_mix = sum(
            (
                kernels[..., tap_idx : tap_idx + 1] * conv_pad[:, tap_idx : tap_idx + LEN]
                for tap_idx in range(KERNEL)
            )
        ).reshape(num_rows, attend)
        query_low = queries.astype(jnp.bfloat16)
        context, log_total = lax.map(
            attend_forward,
            (heads_four(query_low), heads_four(key_low), heads_four(value_low), key_valid),
        )
        joined = jnp.concatenate([context.reshape(num_rows, attend), conv_mix], axis=1).astype(
            jnp.bfloat16
        )
        resid_one = layer_input + product(joined, w_out[layer_number]) + b_out[layer_number]
        normed = norm_rows(resid_one, first_gain[layer_number], first_shift[layer_number])
        normed_low = normed.astype(jnp.bfloat16).reshape(num_rows, 2, half_width)
        group_rows = lax.all_to_all(
            normed_low, "grp", split_axis=1, concat_axis=0, tiled=True
        ).reshape(2 * num_rows, half_width)
        up_full, down_full, bias_full = gather_turned(
            (w_up[layer_number, 0], down_weight[layer_number, 0], b_up[layer_number, 0]),
            CH,
            (1, 0, 0),
        )
        pre_act = product(group_rows, up_full) + bias_full.astype(jnp.float32)
        grouped_output = product(exact_gelu(pre_act).astype(jnp.bfloat16), down_full)
        weights_kept = (up_full, down_full, pre_act)
        back_rows = lax.all_to_all(
            grouped_output.astype(jnp.bfloat16).reshape(2 * num_rows, 1, half_width),
            "grp",
            split_axis=0,
            concat_axis=1,
            tiled=True,
        ).reshape(num_rows, model_width)
        resid_two = normed + back_rows.astype(jnp.float32) + b_down[layer_number]
        result = (
            norm_rows(resid_two, second_gain[layer_number], second_shift[layer_number]) * valid_rows
        )
        kept = {
            "layer_input": layer_input,
            "queries": queries,
            "key_low": key_low,
            "value_low": value_low,
            "depth_low": depth_low,
            "key_conv": key_conv,
            "conv_pad": conv_pad,
            "log_total": log_total,
            "joined": joined,
            "resid_one": resid_one,
            "group_rows": group_rows,
            "weights": weights_kept,
            "resid_two": resid_two,
        }
        return (result, kept)

    def backward_layer(grad_out, layer_number, kept):
        pull_two = jax.vjp(
            norm_rows, kept["resid_two"], second_gain[layer_number], second_shift[layer_number]
        )[1]
        d_resid_two, d_gain_two, d_shift_two = pull_two(grad_out * valid_rows)
        d_bdown = jnp.sum(d_resid_two, axis=0)
        d_send = d_resid_two.astype(jnp.bfloat16).reshape(num_rows, 2, half_width)
        d_group = lax.all_to_all(d_send, "grp", split_axis=1, concat_axis=0, tiled=True).reshape(
            2 * num_rows, half_width
        )
        group_rows = kept["group_rows"]
        up_full, down_full, pre_act = kept["weights"]
        gelu_out, gelu_pull = jax.vjp(exact_gelu, pre_act)
        d_pre = gelu_pull(product_t(d_group, down_full))[0].astype(jnp.bfloat16)
        d_rows = product_t(d_pre, up_full)
        d_up, d_down, d_upbias = (
            summed_rows(inner_rows(group_rows, d_pre), (("ch_0", "ch_1", "ch_2"), "ch_3"), 1),
            *side_by_side(
                (inner_rows(gelu_out.astype(jnp.bfloat16), d_group), column_sum(d_pre)),
                (("ch_0", "ch_1", "ch_2"), "ch_3"),
                0,
                1,
            ),
        )
        d_back = (
            lax.all_to_all(
                d_rows.reshape(2 * num_rows, 1, half_width).astype(jnp.bfloat16),
                "grp",
                split_axis=0,
                concat_axis=1,
                tiled=True,
            )
            .astype(jnp.float32)
            .reshape(num_rows, model_width)
        )
        pull_one = jax.vjp(
            norm_rows, kept["resid_one"], first_gain[layer_number], first_shift[layer_number]
        )[1]
        d_resid_one, d_gain_one, d_shift_one = pull_one(d_resid_two + d_back)
        d_proj = d_resid_one.astype(jnp.bfloat16)
        d_wout = inner_rows(kept["joined"], d_proj)
        d_bout = column_sum(d_proj)
        d_joined = product_t(d_proj, w_out[layer_number]).astype(jnp.bfloat16)
        d_context = heads_four(d_joined[:, :attend])
        d_mix = heads_four(d_joined[:, attend:].astype(jnp.float32))
        queries = kept["queries"]
        query_low = queries.astype(jnp.bfloat16)
        d_query_att, d_key, d_value = lax.map(
            attend_backward,
            (
                heads_four(query_low),
                heads_four(kept["key_low"]),
                heads_four(kept["value_low"]),
                d_context,
                kept["log_total"],
                key_valid,
            ),
        )
        d_query_att = d_query_att.reshape(num_rows, attend)
        d_key = d_key.reshape(num_rows, attend)
        d_value = d_value.reshape(num_rows, attend)
        key_conv = kept["key_conv"]
        mixed, kernels = conv_kernels(queries, key_conv, layer_number)
        conv_pad = kept["conv_pad"]
        d_kernels = jnp.stack(
            [
                jnp.sum(d_mix * conv_pad[:, tap_idx : tap_idx + LEN], axis=-1)
                for tap_idx in range(KERNEL)
            ],
            axis=-1,
        )
        d_conv_pad = sum(
            (
                jnp.pad(
                    kernels[..., tap_idx : tap_idx + 1] * d_mix,
                    ((0, 0), (tap_idx, 2 * conv_reach - tap_idx), (0, 0), (0, 0)),
                )
                for tap_idx in range(KERNEL)
            )
        )
        d_conv = (
            d_conv_pad[:, conv_reach : conv_reach + LEN]
            .reshape(num_rows, attend)
            .astype(jnp.bfloat16)
        )
        d_logit = (
            (kernels * (d_kernels - jnp.sum(kernels * d_kernels, axis=-1, keepdims=True)))
            .reshape(num_rows, HEADS * KERNEL)
            .astype(jnp.bfloat16)
        )
        d_wkernel = inner_rows(mixed.astype(jnp.bfloat16), d_logit)
        d_bkernel = column_sum(d_logit)
        d_mixed = product_t(d_logit, w_kernel[layer_number])
        d_keyconv = (d_mixed * queries).astype(jnp.bfloat16)
        d_query = (d_query_att + d_mixed * key_conv).astype(jnp.bfloat16)
        d_wpoint = inner_rows(kept["depth_low"], d_keyconv)
        d_bkeyconv = column_sum(d_keyconv)
        d_depth = rows_three(product_t(d_keyconv, w_point[layer_number]))
        x_low = kept["layer_input"].astype(jnp.bfloat16)
        x_pad = pad_rows(rows_three(x_low)).astype(jnp.float32)
        d_wdepth = jnp.stack(
            [
                jnp.sum(d_depth * x_pad[:, tap_idx : tap_idx + LEN], axis=(0, 1))
                for tap_idx in range(KERNEL)
            ]
        )
        depth_taps = w_depth[layer_number].astype(jnp.float32)
        d_extended = sum(
            (
                jnp.pad(
                    depth_taps[tap_idx] * d_depth,
                    ((0, 0), (tap_idx, 2 * conv_reach - tap_idx), (0, 0)),
                )
                for tap_idx in range(KERNEL)
            )
        )
        d_input = d_resid_one + d_extended[:, conv_reach : conv_reach + LEN].reshape(
            num_rows, model_width
        )
        d_input = (
            d_input
            + product_t(d_query, w_query[layer_number])
            + product_t(d_key, w_key[layer_number])
        )
        d_input = (
            d_input
            + product_t(d_value, w_value[layer_number])
            + product_t(d_conv, w_conv[layer_number])
        )
        layer_grads = (
            inner_rows(x_low, d_query),
            column_sum(d_query),
            inner_rows(x_low, d_key),
            inner_rows(x_low, d_value),
            column_sum(d_value),
            d_wdepth,
            d_wpoint,
            d_bkeyconv,
            d_wkernel,
            d_bkernel,
            inner_rows(x_low, d_conv),
            column_sum(d_conv),
            d_wout,
            d_bout,
            d_gain_one,
            d_shift_one,
            d_bdown,
            d_gain_two,
            d_shift_two,
        )
        return (d_input, layer_grads, (d_up, d_upbias, d_down))

    current = start_x
    kept_all = []
    for layer_number in range(LAYERS):
        current, kept = forward_layer(current, layer_number)
        kept_all.append(kept)
    grad_flow = cotangent.astype(jnp.float32)
    shared = [None] * LAYERS
    sharded = [None] * LAYERS
    seg_local = jnp.zeros_like(seg_table)
    for layer_number in reversed(range(LAYERS)):
        grad_flow, layer_grads, group_grads = backward_layer(
            grad_flow, layer_number, kept_all[layer_number]
        )
        sharded[layer_number] = group_grads
        if layer_number == 0:
            grad_flow = grad_flow * valid_rows
            seg_local = jnp.stack(
                [
                    jnp.sum(jnp.where(second_seg, 0.0, grad_flow), axis=0),
                    jnp.sum(jnp.where(second_seg, grad_flow, 0.0), axis=0),
                ]
            )
        shared[layer_number] = layer_grads
    stacked = tuple(
        (
            jnp.stack([shared[layer_pos][member] for layer_pos in range(LAYERS)])
            for member in range(19)
        )
    )
    totals = lax.psum(stacked + (seg_local,), GRP_CH)
    grad_up = jnp.stack([sharded[layer_pos][0] for layer_pos in range(LAYERS)])[:, None]
    grad_upbias = jnp.stack([sharded[layer_pos][1] for layer_pos in range(LAYERS)])[:, None]
    grad_down = jnp.stack([sharded[layer_pos][2] for layer_pos in range(LAYERS)])[:, None]
    return (
        current,
        grad_flow,
        totals[19],
        totals[0],
        totals[1],
        totals[2],
        totals[3],
        totals[4],
        totals[5],
        totals[6],
        totals[7],
        totals[8],
        totals[9],
        totals[10],
        totals[11],
        totals[12],
        totals[13],
        totals[14],
        totals[15],
        grad_up,
        grad_upbias,
        grad_down,
        totals[16],
        totals[17],
        totals[18],
    )


def solution(mesh):
    finer = Mesh(
        mesh.devices.reshape(mesh.shape["grp"], 4, 4, 2, 2), ("grp", "ch_0", "ch_1", "ch_2", "ch_3")
    )
    placed = (
        P(GRP_CH, None),
        P(GRP_CH, None),
        P(),
        P(),
        P(),
        P(),
        P(),
        P(),
        P(),
        P(),
        P(),
        P(),
        P(),
        P(),
        P(),
        P(),
        P(),
        P(),
        P(),
        P(),
        P(),
        P(None, "grp", None, CH),
        P(None, "grp", CH),
        P(None, "grp", CH, None),
        P(),
        P(),
        P(),
    )
    return jax.shard_map(
        shards,
        mesh=finer,
        in_specs=placed,
        out_specs=(
            P(GRP_CH, None),
            P(GRP_CH, None),
            P(),
            P(),
            P(),
            P(),
            P(),
            P(),
            P(),
            P(),
            P(),
            P(),
            P(),
            P(),
            P(),
            P(),
            P(),
            P(),
            P(),
            P(None, "grp", None, CH),
            P(None, "grp", CH),
            P(None, "grp", CH, None),
            P(),
            P(),
            P(),
        ),
        check_vma=False,
    )
```

profile of v0, /device:TPU:1, one launch (start us, length us, event | category | flops | bytes accessed | tf_op | source)
XLA Modules:
  0.0 1077.5 jit_solution(8421198910530771093)
XLA Ops:
  46.8 5.7 all-to-all-start
  52.5 68.0 %all-gather.3.cloned.1.call-done = bf16[1536,769]{1,0:T(8,128)(2,1)} async-done(((bf16[24,769]{1,0:T(8,128)(2,1)}), bf16[1536,769]{1,0:T(8,128)(2,1)}) %all-gather.3.cloned.1.call-update) | async-done | bytes 2362384 | tf_op jit(solution)/shard_map/all_gather | solution.py:24
  121.7 15.6 %fusion = (f32[1024,1536]{1,0:T(8,128)S(1)}, f32[1024,1536]{1,0:T(8,128)S(1)}) fusion(f32[1536]{0:T(1024)S(1)} %convert_reduce_fusion.5, bf16[1024,384]{1,0:T(8,128)(2,1)S(1)} %bitcast.876, bf16[1536,769]{1,0:T(8,128)(2,1)} %all-gather.3.cloned.1.call-done), kind=kOutput, calls=%fused_computation.4 | convolution fusion | flops 1307049984 | bytes 14555136 | tf_op jit(solution)/shard_map/dot_general | solution.py:70
  153.7 9.8 all-to-all-done.1
  209.0 50.6 %all-gather.5.cloned.1.call-done = bf16[1536,769]{1,0:T(8,128)(2,1)} async-done(((bf16[24,769]{1,0:T(8,128)(2,1)}), bf16[1536,769]{1,0:T(8,128)(2,1)}) %all-gather.5.cloned.1.call-update) | async-done | bytes 2362384 | tf_op jit(solution)/shard_map/all_gather | solution.py:24
  260.8 15.7 %fusion.1 = (f32[1024,1536]{1,0:T(8,128)S(1)}, f32[1024,1536]{1,0:T(8,128)S(1)}) fusion(f32[1536]{0:T(1024)S(1)} %convert_reduce_fusion.4, bf16[1024,384]{1,0:T(8,128)(2,1)} %bitcast.50, bf16[1536,769]{1,0:T(8,128)(2,1)} %all-gather.5.cloned.1.call-done), kind=kOutput, calls=%fused_computation.5 | convolution fusion | flops 1307049984 | bytes 14555136 | tf_op jit(solution)/shard_map/dot_general | solution.py:70
  294.3 16.4 %fusion.21 = (bf16[1536,1024]{0,1:T(8,128)(2,1)}, f32[1536,1024]{0,1:T(8,128)}) fusion(f32[1024,1536]{1,0:T(8,128)} %copy-done.8, f32[1536]{0:T(1024)S(1)} %copy-done.168), kind=kLoop, calls=%fused_computation.39 | loop fusion | flops 103809024 | bytes 15734784 | tf_op jit(solution)/shard_map/convert_element_type | solution.py:245
  339.0 16.2 %fusion.12 = (bf16[1536,1024]{0,1:T(8,128)(2,1)}, f32[1536,1024]{0,1:T(8,128)}) fusion(f32[1024,1536]{1,0:T(8,128)} %copy-done.9, f32[1536]{0:T(1024)} %copy-done.171), kind=kLoop, calls=%fused_computation.23 | loop fusion | flops 103809024 | bytes 15734784 | tf_op jit(solution)/shard_map/convert_element_type | solution.py:245
  363.7 11.9 %convert_reduce_fusion = (f32[1536]{0:T(1024)}, bf16[1024,1536]{1,0:T(8,128)(2,1)S(1)}, f32[1024,1536]{1,0:T(8,128)}) fusion(f32[1024,1536]{1,0:T(8,128)} %copy-done.30, f32[1024,1536]{1,0:T(8,128)} %copy-done.9, f32[1536]{0:T(1024)} %copy-done.171, bf16[1024,384]{1,0:T(8,128)(2,1)} %bitcast.60, bf16[1536,769]{1,0:T(8,128)(2,1)} %all-gather.5.cloned.1.call-done), kind=kOutput, calls=%fused_computation.40 | convolution fusion | flops 1234696704 | bytes 24000512 | tf_op jit(solution)/shard_map/dot_general | solution.py:74
  388.7 9.8 fusion.10
  441.2 5.9 multiply_reduce_fusion.23
  497.3 11.9 %convert_reduce_fusion.1 = (f32[1536]{0:T(1024)}, bf16[1024,1536]{1,0:T(8,128)(2,1)S(1)}, f32[1024,1536]{1,0:T(8,128)}) fusion(f32[1024,1536]{1,0:T(8,128)} %copy-done.29, f32[1024,1536]{1,0:T(8,128)} %copy-done.8, f32[1536]{0:T(1024)S(1)} %copy-done.169, bf16[1024,384]{1,0:T(8,128)(2,1)} %bitcast.85, bf16[1536,769]{1,0:T(8,128)(2,1)} %all-gather.3.cloned.1.call-done), kind=kOutput, calls=%fused_computation.41 | convolution fusion | flops 1234696704 | bytes 23998464 | tf_op jit(solution)/shard_map/dot_general | solution.py:74
  522.6 6.2 all-to-all-done.7
  528.8 8.0 all-to-all-start.10
  562.1 5.9 multiply_reduce_fusion.14
  670.3 7.9 fusion.19
  692.6 6.5 all_to_all.136
  699.1 6.2 all_to_all.137
  705.3 5.4 all-to-all-start.11
  714.3 14.9 %all-to-all-done.11 = f32[32,384,24]{1,2,0:T(8,128)} async-done(((f32[32,384,24]{1,2,0:T(8,128)}), f32[32,384,24]{1,2,0:T(8,128)}, u32[]{:S(2)}, u32[]{:S(2)}) %all-to-all-start.11) | async-done | bytes 1179680 | tf_op jit(solution)/shard_map/all_to_all | solution.py:48
  736.9 19.1 %all-to-all-done.15 = f32[32,24,385]{2,1,0:T(8,128)} async-done(((f32[32,24,385]{2,1,0:T(8,128)}), f32[32,24,385]{2,1,0:T(8,128)}, u32[]{:S(2)}, u32[]{:S(2)}) %all-to-all-start.15) | async-done | bytes 1182752 | tf_op jit(solution)/shard_map/all_to_all | solution.py:48
  762.3 14.8 %all-to-all-done.9 = f32[32,384,24]{1,2,0:T(8,128)} async-done(((f32[32,384,24]{1,2,0:T(8,128)}), f32[32,384,24]{1,2,0:T(8,128)}, u32[]{:S(2)}, u32[]{:S(2)}) %all-to-all-start.9) | async-done | bytes 1179680 | tf_op jit(solution)/shard_map/all_to_all | solution.py:48
  784.5 37.4 %all-reduce.45.cloned.1.call-done = (f32[2,768]{1,0:T(2,128)}, f32[2,384]{1,0:T(2,128)}, f32[2,384]{1,0:T(2,128)}, f32[2,9,768]{2,1,0:T(8,128)}, f32[2,384]{1,0:...) async-done(((f32[2,768]{1,0:T(2,128)}, f32[2,384]{1,0:T(2,128)}, ...) | async-done | bytes 111040 | tf_op jit(solution)/shard_map/psum | solution.py:456
  826.9 222.8 %all-reduce.47.cloned.1.call-done = (f32[2,768,384]{2,1,0:T(8,128)}, f32[2,768,384]{2,1,0:T(8,128)}, f32[2,768,384]{2,1,0:T(8,128)}, f32[2,768,384]{2,1,0:T(8,12...) async-done(((f32[2,768,384]{2,1,0:T(8,128)}, f32[2,768,384]{2,1,0:T(8,128)}, f32[2,768,384]{2,1,0:T(8,128)}, f32[2,768,384]{2,1,0:T(8,128)}, ...) | async-done | bytes 16680976 | tf_op jit(solution)/shard_map/psum | solution.py:456
  (1054 shorter events, 466.5 us)
Async XLA Ops:
  7.3 113.2 %all-gather.3.cloned.1.call-start = ((), (), s32[]{:S(2)}) async-start(), calls=%async_computation.16 | async-start | bytes 2795520 | tf_op jit(solution)/shard_map/all_gather | solution.py:24
  30.9 175.9 %copy-start.124 = (f32[512,6]{0,1:T(8,128)}, f32[512,6]{0,1:T(8,128)S(1)}, u32[]{:S(2)}) copy-start(f32[512,6]{0,1:T(8,128)S(1)} %reduce_max.43) | copy-start | bytes 36868
  33.0 132.7 %copy-start.179 = (f32[768]{0:T(1024)}, f32[768]{0:T(1024)S(1)}, u32[]{:S(2)}) copy-start(f32[768]{0:T(1024)S(1)} %get-tuple-element.503) | copy-start | bytes 9220
  45.2 120.6 %copy-start.187 = (f32[512]{0:T(512)}, f32[512]{0:T(512)S(1)}, u32[]{:S(2)}) copy-start(f32[512]{0:T(512)S(1)} %broadcast_multiply_fusion.21) | copy-start | bytes 6148
  45.5 120.3 %copy-start.201 = (f32[512]{0:T(512)}, f32[512]{0:T(512)S(1)}, u32[]{:S(2)}) copy-start(f32[512]{0:T(512)S(1)} %fusion.198) | copy-start | bytes 6148
  46.8 74.9 %all-to-all-start = ((bf16[512,2,384]{2,0,1:T(8,128)(2,1)}), bf16[512,2,384]{2,0,1:T(8,128)(2,1)S(1)}, u32[]{:S(2)}, u32[]{:S(2)}) async-start(bf16[512,2,384]{2,0,1:T(8,128)(2,1)} %bitcast.784), calls=%async_computation | async-start | bytes 1572864 | tf_op jit(solution)/shard_map/all_to_all | solution.py:236
  147.7 15.7 %all-to-all-start.1 = ((bf16[2,2,98304]{2,1,0:T(2,128)(2,1)}), bf16[2,2,98304]{2,1,0:T(2,128)(2,1)S(1)}, u32[]{:S(2)}, u32[]{:S(2)}) async-start(bf16[2,2,98304]{2,1,0:T(2,128)(2,1)} %reshape.1479), calls=%async_computation.1 | async-start | bytes 1572864 | tf_op jit(solution)/shard_map/all_to_all | solution.py:247
  151.7 107.9 %all-gather.5.cloned.1.call-start = ((), (), s32[]{:S(2)}) async-start(), calls=%async_computation.17 | async-start | bytes 2795520 | tf_op jit(solution)/shard_map/all_gather | solution.py:24
  199.4 61.4 %all-to-all-start.2 = ((bf16[512,2,384]{2,0,1:T(8,128)(2,1)}), bf16[512,2,384]{2,0,1:T(8,128)(2,1)}, u32[]{:S(2)}, u32[]{:S(2)}) async-start(bf16[512,2,384]{2,0,1:T(8,128)(2,1)} %bitcast.843), calls=%async_computation.2 | async-start | bytes 1572864 | tf_op jit(solution)/shard_map/all_to_all | solution.py:236
  290.0 30.8 %all-to-all-start.3 = ((bf16[2,2,98304]{2,1,0:T(2,128)(2,1)}), bf16[2,2,98304]{2,1,0:T(2,128)(2,1)}, u32[]{:S(2)}, u32[]{:S(2)}) async-start(bf16[2,2,98304]{2,1,0:T(2,128)(2,1)} %reshape.1481), calls=%async_computation.3 | async-start | bytes 1572864 | tf_op jit(solution)/shard_map/all_to_all | solution.py:247
  334.7 29.0 %all-to-all-start.4 = ((bf16[512,2,384]{2,0,1:T(8,128)(2,1)}), bf16[512,2,384]{2,0,1:T(8,128)(2,1)}, u32[]{:S(2)}, u32[]{:S(2)}) async-start(bf16[512,2,384]{2,0,1:T(8,128)(2,1)} %bitcast.842), calls=%async_computation.4 | async-start | bytes 1572864 | tf_op jit(solution)/shard_map/all_to_all | solution.py:282
  384.4 24.3 %all-to-all-start.5 = ((bf16[2,2,98304]{2,1,0:T(2,128)(2,1)}), bf16[2,2,98304]{2,1,0:T(2,128)(2,1)}, u32[]{:S(2)}, u32[]{:S(2)}) async-start(bf16[2,2,98304]{2,1,0:T(2,128)(2,1)} %reshape.1483), calls=%async_computation.5 | async-start | bytes 1572864 | tf_op jit(solution)/shard_map/all_to_all | solution.py:300
  481.8 15.4 %all-to-all-start.6 = ((bf16[512,2,384]{2,0,1:T(8,128)(2,1)}), bf16[512,2,384]{2,0,1:T(8,128)(2,1)}, u32[]{:S(2)}, u32[]{:S(2)}) async-start(bf16[512,2,384]{2,0,1:T(8,128)(2,1)} %bitcast.781), calls=%async_computation.6 | async-start | bytes 1572864 | tf_op jit(solution)/shard_map/all_to_all | solution.py:282
  514.3 14.4 %all-to-all-start.7 = ((bf16[2,2,98304]{2,1,0:T(2,128)(2,1)}), bf16[2,2,98304]{2,1,0:T(2,128)(2,1)S(1)}, u32[]{:S(2)}, u32[]{:S(2)}) async-start(bf16[2,2,98304]{2,1,0:T(2,128)(2,1)} %reshape.1485), calls=%async_computation.7 | async-start | bytes 1572864 | tf_op jit(solution)/shard_map/all_to_all | solution.py:300
  528.8 133.2 %all-to-all-start.10 = ((f32[2,32,384,24]{2,3,1,0:T(8,128)}), f32[2,32,384,24]{2,3,1,0:T(8,128)}, u32[]{:S(2)}, u32[]{:S(2)}) async-start(f32[2,32,384,24]{2,3,1,0:T(8,128)} %bitcast.779), calls=%async_computation.10 | async-start | bytes 4718592 | tf_op jit(solution)/shard_map/all_to_all | solution.py:40
  536.8 285.1 %all-reduce.45.cloned.1.call-start = ((), (), s32[]{:S(2)}) async-start(), calls=%async_computation.18 | async-start | bytes 309248 | tf_op jit(solution)/shard_map/psum | solution.py:456
  598.4 36.4 %copy-start.31 = (f32[1,768,384]{2,1,0:T(8,128)S(1)}, f32[1,768,384]{2,1,0:T(8,128)}, u32[]{:S(2)}) copy-start(f32[1,768,384]{2,1,0:T(8,128)} %convolution_bitcast_fusion.10) | copy-start | bytes 3538948
  650.2 399.4 %all-reduce.47.cloned.1.call-start = ((), (), s32[]{:S(2)}) async-start(), calls=%async_computation.19 | async-start | bytes 33374208 | tf_op jit(solution)/shard_map/psum | solution.py:456
  662.0 30.6 %all-to-all-start.14 = ((f32[2,32,24,385]{3,2,1,0:T(8,128)}), f32[2,32,24,385]{3,2,1,0:T(8,128)}, u32[]{:S(2)}, u32[]{:S(2)}) async-start(f32[2,32,24,385]{3,2,1,0:T(8,128)} %copy.245), calls=%async_computation.14 | async-start | bytes 6291456 | tf_op jit(solution)/shard_map/all_to_all | solution.py:40
  705.3 23.9 %all-to-all-start.11 = ((f32[32,384,24]{1,2,0:T(8,128)}), f32[32,384,24]{1,2,0:T(8,128)}, u32[]{:S(2)}, u32[]{:S(2)}) async-start(f32[32,384,24]{1,2,0:T(8,128)} %reduce_sum.1034), calls=%async_computation.11 | async-start | bytes 2359296 | tf_op jit(solution)/shard_map/all_to_all | solution.py:48
  729.2 26.8 %all-to-all-start.15 = ((f32[32,24,385]{2,1,0:T(8,128)}), f32[32,24,385]{2,1,0:T(8,128)}, u32[]{:S(2)}, u32[]{:S(2)}) async-start(f32[32,24,385]{2,1,0:T(8,128)} %reduce_sum.1040), calls=%async_computation.15 | async-start | bytes 3145728 | tf_op jit(solution)/shard_map/all_to_all | solution.py:48
  756.0 21.1 %all-to-all-start.9 = ((f32[32,384,24]{1,2,0:T(8,128)}), f32[32,384,24]{1,2,0:T(8,128)}, u32[]{:S(2)}, u32[]{:S(2)}) async-start(f32[32,384,24]{1,2,0:T(8,128)} %reduce_sum.1032), calls=%async_computation.9 | async-start | bytes 2359296 | tf_op jit(solution)/shard_map/all_to_all | solution.py:48
  777.1 48.3 %all-to-all-start.13 = ((f32[32,24,385]{2,1,0:T(8,128)}), f32[32,24,385]{2,1,0:T(8,128)S(1)}, u32[]{:S(2)}, u32[]{:S(2)}) async-start(f32[32,24,385]{2,1,0:T(8,128)} %reduce_sum.1037), calls=%async_computation.13 | async-start | bytes 3145728 | tf_op jit(solution)/shard_map/all_to_all | solution.py:48
  821.9 229.4 %copy-start.296 = (f32[2,768]{1,0:T(2,128)S(1)}, f32[2,768]{1,0:T(2,128)}, u32[]{:S(2)}) copy-start(f32[2,768]{1,0:T(2,128)} %get-tuple-element.509) | copy-start | bytes 18436
  (326 other events, 1165.4 us)
Sparse Core Ops, SparseCore 0:
  12.1 108.3 all-gather.2
  154.8 104.7 all-gather.4
  650.3 171.5 all-reduce.44
  829.3 220.2 all-reduce.46
where the time goes:
time: 1090 us; the launch traced here: 1080 us
  waiting for transfers between devices  444 us (41%)
  local copies, waits for them, and re-layouts  187 us (17%)
  other arithmetic  178 us (16%)
  matrix products  169 us (16%)
  starting transfers between devices  68.8 us (6%)
  between operations  18.4 us (2%)
  blocking collectives  12.7 us (1%)
    psum x2, waiting for transfers between devices, shards(): totals = lax.psum(stacked + (seg_local,), GRP_CH)  260 us
    all_gather x2, waiting for transfers between devices, gather_turned(): lax.all_gather(both, axis, axis=0, tiled=True)  119 us
    unnamed x716, local copies, waits for them, and re-layouts  78.5 us
    dot_general x18, matrix products, product_t(): lax.dot_general(first_op, second_op, (((1,), (1,)), ((), ())), preferred_...  52.6 us
    dot_general x18, matrix products, product(): return jnp.dot(first_op, second_op, preferred_element_type=jnp.float32)  51.9 us
    all_to_all x4, waiting for transfers between devices, summed_rows(): lax.all_to_all(nearer, far, split_axis=0, concat_axis=0, tiled=True)  48.8 us
    dot_general x18, matrix products, inner_rows(): lax.dot_general(first_op, second_op, (((0,), (0,)), ((), ())), preferred_...  38.3 us
    convert_element_type x2, other arithmetic, forward_layer(): exact_gelu(pre_act).astype(jnp.bfloat16)  32.6 us
  transfers between devices with their start and end apart: 18, of which 9 were waited for; matrix products, arithmetic and copies ran while one was open for 29% of the time, Pallas kernels for 0%

commit v1 on v0

--- a/solution.py
+++ b/solution.py
@@ -1,6 +1,10 @@
+import functools
+
 import jax
 import jax.numpy as jnp
 from jax import lax
+from jax.experimental import pallas as pl
+from jax.experimental.pallas import tpu as pltpu
 from jax.sharding import Mesh
 from jax.sharding import PartitionSpec as P
 
@@ -18,46 +22,339 @@
 MASK_VALUE = -1000000000.0
 
 
-def gather_turned(arrays, axis, dims):
-    turned = [jnp.moveaxis(a, dim, 0) for a, dim in zip(arrays, dims)]
-    both = jnp.concatenate([t.reshape(len(t), -1) for t in turned], axis=1)
-    whole, at, finished = (lax.all_gather(both, axis, axis=0, tiled=True), 0, [])
-    for t, dim in zip(turned, dims):
-        piece = whole[:, at : at + t[0].size].reshape(-1, *t.shape[1:])
-        finished.append(jnp.moveaxis(piece, 0, dim))
-        at += t[0].size
-    return tuple(finished)
-
-
-def cut_along(x, dim, length):
-    shape = x.shape
-    tiles = x.reshape(*shape[:dim], length, shape[dim] // length, *shape[dim + 1 :])
-    return jnp.moveaxis(tiles, dim, 0)
-
-
-def summed_on_arrival(x, axis, dim):
-    tiles = cut_along(x, dim, lax.axis_size(axis))
-    arrived = lax.all_to_all(tiles, axis, split_axis=0, concat_axis=0, tiled=True)
-    return arrived.sum(axis=0)
-
-
-def summed_rows(x, axes, dim):
-    far, near = axes
-    tiles = cut_along(x, dim, lax.axis_size(far))
-    nearer = summed_on_arrival(tiles, near, dim + 1)
-    arrived = lax.all_to_all(nearer, far, split_axis=0, concat_axis=0, tiled=True)
-    return arrived.sum(axis=0)
-
-
-def side_by_side(arrays, axis, dim, along):
-    columns = [a.reshape(*a.shape[:along], -1) for a in arrays]
-    both = jnp.concatenate(columns, axis=along)
-    whole, at, finished = (summed_rows(both, axis, dim), 0, [])
-    for a, column in zip(arrays, columns):
-        piece = whole[..., at : at + column.shape[along]]
-        finished.append(piece.reshape(*piece.shape[:along], *a.shape[along:]))
-        at += column.shape[along]
-    return tuple(finished)
+MESH = pl.DeviceIdType.MESH
+LANES = 384
+PARTS = 3
+ORDERS = ("xyz", "yzx", "zxy")
+
+
+def here():
+    x, y = lax.axis_index("ch_1"), lax.axis_index("ch_0")
+    z = lax.axis_index("grp") * 2 + lax.axis_index("ch_2")
+    return {"x": x, "y": y, "z": z, "core": lax.axis_index("ch_3")}
+
+
+def device_at(axis, place):
+    if axis == "x":
+        return {"ch_1": place}
+    if axis == "y":
+        return {"ch_0": place}
+    if axis == "z":
+        return {"grp": place // 2, "ch_2": place % 2}
+    return {"ch_3": place}
+
+
+def greet(at):
+    barrier = pltpu.get_barrier_semaphore()
+    peers = [("core", 1 - at["core"])]
+    for axis in "xyz":
+        peers += [(axis, (at[axis] + 1) % 4), (axis, (at[axis] + 3) % 4)]
+    for axis, place in peers:
+        pl.semaphore_signal(barrier, inc=1, device_id=device_at(axis, place), device_id_type=MESH)
+    pl.semaphore_wait(barrier, len(peers))
+
+
+class Sends:
+    def __init__(self, send_sems, recv_sems):
+        self.send_sems, self.recv_sems, self.count, self.all = send_sems, recv_sems, 0, []
+
+    def start(self, src, dst, axis, place):
+        copy = pltpu.make_async_remote_copy(
+            src_ref=src, dst_ref=dst,
+            send_sem=self.send_sems.at[self.count], recv_sem=self.recv_sems.at[self.count],
+            device_id=device_at(axis, place), device_id_type=MESH)
+        self.count += 1
+        copy.start()
+        self.all.append(copy)
+        return copy
+
+    def finish(self):
+        for copy in self.all:
+            copy.wait_send()
+
+
+def add_into(dst, *srcs):
+    lead = dst.shape[:-2]
+    total = 1
+    for n in lead:
+        total *= n
+
+    def one(i):
+        idx, rest = [], i
+        for n in reversed(lead):
+            idx.append(rest % n)
+            rest = rest // n
+        idx = tuple(reversed(idx))
+        acc = dst[idx].astype(jnp.float32) if idx else dst[...].astype(jnp.float32)
+        for s in srcs:
+            acc = acc + (s[idx] if idx else s[...]).astype(jnp.float32)
+        if idx:
+            dst[idx] = acc.astype(jnp.bfloat16)
+        else:
+            dst[...] = acc.astype(jnp.bfloat16)
+
+    if total == 1 and not lead:
+        one(0)
+    else:
+        pl.loop(0, total)(one)
+
+
+def halves(ref):
+    n = ref.shape[0] // 2
+    return ref.at[pl.ds(0, n)], ref.at[pl.ds(n, n)]
+
+
+class Scatter:
+    def __init__(self, at, sends, x, sums, core_in, bufs):
+        self.at, self.sends, self.x, self.sums, self.core_in, self.bufs = at, sends, x, sums, core_in, bufs
+
+    def places(self, p, s):
+        axis = ORDERS[p][s]
+        i = self.at[axis]
+        return axis, i, (i + 1) % 4, (i + 2) % 4, (i + 3) % 4
+
+    def begin(self):
+        c = self.at["core"]
+        self.core = {}
+        for turn in (2, 1, 3, 0):
+            for p in range(PARTS):
+                k = (self.at[ORDERS[p][0]] + turn) % 4
+                self.core[p, turn] = self.sends.start(
+                    self.x.at[p, 1 - c, k], self.core_in.at[p, k], "core", 1 - c)
+
+    def arrive(self, p, turn):
+        k = (self.at[ORDERS[p][0]] + turn) % 4
+        self.core[p, turn].wait_recv()
+        add_into(self.sums.at[p, k], self.core_in.at[p, k])
+
+    def block(self, p, s, k):
+        if s == 0:
+            return self.sums.at[p, k]
+        if s == 1:
+            return self.sums.at[p, self.at[ORDERS[p][0]], k]
+        return self.sums.at[p, self.at[ORDERS[p][0]], self.at[ORDERS[p][1]], k]
+
+    def split(self, s):
+        return s < 2 or self.x.shape[-2] % 32 == 0
+
+    def first(self, p, s):
+        axis, i, up, far, down = self.places(p, s)
+        t = self.bufs[s].at[p, 0]
+        src = self.block(p, s, far)
+        if self.split(s):
+            (s0, s1), (t0, t1) = halves(src), halves(t)
+            return (self.sends.start(s0, t0, axis, up), self.sends.start(s1, t1, axis, down))
+        return (self.sends.start(src, t, axis, up),)
+
+    def second_early(self, p, s):
+        axis, i, up, far, down = self.places(p, s)
+        u0, u1 = self.bufs[s].at[p, 1], self.bufs[s].at[p, 2]
+        if self.split(s):
+            a = self.sends.start(halves(self.block(p, s, up))[1], halves(u0)[1], axis, up)
+            b = self.sends.start(halves(self.block(p, s, down))[0], halves(u1)[0], axis, down)
+            return [a, b]
+        return [self.sends.start(self.block(p, s, down), u1, axis, down)]
+
+    def second_late(self, p, s, firsts):
+        axis, i, up, far, down = self.places(p, s)
+        t, u0, u1 = (self.bufs[s].at[p, n] for n in range(3))
+        out = []
+        if self.split(s):
+            firsts[0].wait_recv()
+            half = halves(self.block(p, s, up))[0]
+            add_into(half, halves(t)[0])
+            out.append(self.sends.start(half, halves(u0)[0], axis, up))
+            firsts[1].wait_recv()
+            half = halves(self.block(p, s, down))[1]
+            add_into(half, halves(t)[1])
+            out.append(self.sends.start(half, halves(u1)[1], axis, down))
+        else:
+            firsts[0].wait_recv()
+            whole = self.block(p, s, up)
+            add_into(whole, t)
+            out.append(self.sends.start(whole, u0, axis, up))
+        return out
+
+    def last(self, p, s, copies):
+        for copy in copies:
+            copy.wait_recv()
+        axis, i, up, far, down = self.places(p, s)
+        add_into(self.block(p, s, i), self.bufs[s].at[p, 1], self.bufs[s].at[p, 2])
+
+    def run(self):
+        self.begin()
+        firsts, seconds = {}, {}
+        for p in range(PARTS):
+            self.arrive(p, 2)
+            firsts[p] = self.first(p, 0)
+        for p in range(PARTS):
+            self.arrive(p, 1)
+            self.arrive(p, 3)
+            seconds[p] = self.second_early(p, 0)
+        for p in range(PARTS):
+            self.arrive(p, 0)
+        for p in range(PARTS):
+            seconds[p] += self.second_late(p, 0, firsts[p])
+        for s in (1, 2):
+            for p in range(PARTS):
+                self.last(p, s - 1, seconds[p])
+                firsts[p] = self.first(p, s)
+                seconds[p] = self.second_early(p, s)
+            for p in range(PARTS):
+                seconds[p] += self.second_late(p, s, firsts[p])
+        for p in range(PARTS):
+            self.last(p, 2, seconds[p])
+
+    def own(self, p):
+        o = ORDERS[p]
+        return self.sums.at[p, self.at[o[0]], self.at[o[1]], self.at[o[2]]]
+
+
+def scatter_scratch(R):
+    bf = jnp.bfloat16
+    return [pltpu.VMEM((PARTS, 4, 4, 4, R, LANES), bf), pltpu.VMEM((PARTS, 4, 4, 4, R, LANES), bf),
+            pltpu.VMEM((PARTS, 3, 4, 4, R, LANES), bf), pltpu.VMEM((PARTS, 3, 4, R, LANES), bf),
+            pltpu.VMEM((PARTS, 3, R, LANES), bf)]
+
+
+class Gather:
+    def __init__(self, at, sends, g):
+        self.at, self.sends, self.g = at, sends, g
+
+    def block(self, p, s, k):
+        c, o = self.at["core"], ORDERS[p]
+        if s == 0:
+            return self.g.at[p, c, k]
+        if s == 1:
+            return self.g.at[p, c, self.at[o[0]], k]
+        return self.g.at[p, c, self.at[o[0]], self.at[o[1]], k]
+
+    def split(self, s):
+        return s < 2 or self.g.shape[-2] % 32 == 0
+
+    def first(self, p, s):
+        axis = ORDERS[p][s]
+        i = self.at[axis]
+        mine = self.block(p, s, i)
+        return (self.sends.start(mine, mine, axis, (i + 1) % 4), self.sends.start(mine, mine, axis, (i + 3) % 4))
+
+    def second(self, p, s, firsts):
+        axis = ORDERS[p][s]
+        i = self.at[axis]
+        firsts[0].wait_recv()
+        low = self.block(p, s, (i + 3) % 4)
+        if not self.split(s):
+            out = [self.sends.start(low, low, axis, (i + 1) % 4)]
+            firsts[1].wait_recv()
+            return out
+        low = halves(low)[0]
+        out = [self.sends.start(low, low, axis, (i + 1) % 4)]
+        firsts[1].wait_recv()
+        high = halves(self.block(p, s, (i + 1) % 4))[1]
+        return out + [self.sends.start(high, high, axis, (i + 3) % 4)]
+
+    def across(self, p, turn):
+        k = (self.at[ORDERS[p][0]] + turn) % 4
+        mine = self.g.at[p, self.at["core"], k]
+        return self.sends.start(mine, mine, "core", 1 - self.at["core"])
+
+    def run(self):
+        firsts, seconds, cores = {}, {}, []
+        for s in (2, 1):
+            for p in range(PARTS):
+                firsts[p] = self.first(p, s)
+            for p in range(PARTS):
+                seconds[p] = self.second(p, s, firsts[p])
+            for p in range(PARTS):
+                for copy in seconds[p]:
+                    copy.wait_recv()
+        for p in range(PARTS):
+            firsts[p] = self.first(p, 0)
+        for p in range(PARTS):
+            cores.append(self.across(p, 0))
+        for p in range(PARTS):
+            seconds[p] = self.second(p, 0, firsts[p])
+            cores.append(self.across(p, 3))
+            cores.append(self.across(p, 1))
+        for p in range(PARTS):
+            for copy in seconds[p]:
+                copy.wait_recv()
+            cores.append(self.across(p, 2))
+        for copy in cores:
+            copy.wait_recv()
+
+
+def exchange_kernel(R, Rg, x, g, own_out, sums, core_in, b0, b1, b2, local, ss, rs):
+    at = here()
+    greet(at)
+    sends = Sends(ss, rs)
+    load = pltpu.make_async_copy(x.at[:, at["core"]], sums, local.at[0])
+    load.start()
+    sc = Scatter(at, sends, x, sums, core_in, (b0, b1, b2))
+    load.wait()
+    sc.run()
+    put = []
+    for p in range(PARTS):
+        own_out[p] = sc.own(p)[...]
+        if Rg:
+            o = ORDERS[p]
+            g[p, at["core"], at[o[0]], at[o[1]], at[o[2]]] = sc.own(p)[pl.ds(R - Rg, Rg)]
+    if Rg:
+        Gather(at, sends, g).run()
+    sends.finish()
+
+
+def exchange(x, R, Rg, cid):
+    bf = jnp.bfloat16
+    return pl.pallas_call(
+        functools.partial(exchange_kernel, R, Rg),
+        out_shape=(jax.ShapeDtypeStruct((PARTS, 2, 4, 4, 4, Rg, LANES), bf),
+                   jax.ShapeDtypeStruct((PARTS, R, LANES), bf)),
+        in_specs=[pl.BlockSpec(memory_space=pl.ANY)],
+        out_specs=(pl.BlockSpec(memory_space=pltpu.VMEM), pl.BlockSpec(memory_space=pltpu.VMEM)),
+        scratch_shapes=scatter_scratch(R) + [pltpu.SemaphoreType.DMA((1,)), pltpu.SemaphoreType.DMA((120,)), pltpu.SemaphoreType.DMA((120,))],
+        compiler_params=pltpu.CompilerParams(collective_id=cid, has_side_effects=True, vmem_limit_bytes=60 << 20),
+    )(x)
+
+
+def gather_kernel(R, own, g, ss, rs):
+    at = here()
+    for p in range(PARTS):
+        o = ORDERS[p]
+        g[p, at["core"], at[o[0]], at[o[1]], at[o[2]]] = own[p]
+    greet(at)
+    sends = Sends(ss, rs)
+    Gather(at, sends, g).run()
+    sends.finish()
+
+
+def gather(own, R, cid):
+    return pl.pallas_call(
+        functools.partial(gather_kernel, R),
+        out_shape=jax.ShapeDtypeStruct((PARTS, 2, 4, 4, 4, R, LANES), jnp.bfloat16),
+        in_specs=[pl.BlockSpec(memory_space=pltpu.VMEM)],
+        out_specs=pl.BlockSpec(memory_space=pltpu.VMEM),
+        scratch_shapes=[pltpu.SemaphoreType.DMA((60,)), pltpu.SemaphoreType.DMA((60,))],
+        compiler_params=pltpu.CompilerParams(collective_id=cid, has_side_effects=True, vmem_limit_bytes=60 << 20),
+    )(own)
+
+
+PLACES = {"xyz": (2, 1, 0, 3), "yzx": (1, 0, 3, 2), "zxy": (0, 3, 2, 1)}
+
+
+def to_part(rows, p):
+    r = rows.shape[1]
+    cut = rows.reshape(2, 4, 4, 2, 2, r, LANES)
+    return jnp.transpose(cut, (4,) + PLACES[ORDERS[p]] + (5, 6)).reshape(2, 4, 4, 4, r, LANES)
+
+
+def from_part(part, p):
+    r = part.shape[-2]
+    order = (4,) + PLACES[ORDERS[p]] + (5, 6)
+    sizes = (2, 4, 4, 2, 2, r, LANES)
+    cut = part.reshape([sizes[d] for d in order])
+    back = [order.index(d) for d in range(7)]
+    return jnp.transpose(cut, back).reshape(128, r, LANES)
 
 
 def norm_rows(residual, gains, offset):
@@ -232,25 +529,18 @@
         )
         resid_one = layer_input + product(joined, w_out[layer_number]) + b_out[layer_number]
         normed = norm_rows(resid_one, first_gain[layer_number], first_shift[layer_number])
-        normed_low = normed.astype(jnp.bfloat16).reshape(num_rows, 2, half_width)
-        group_rows = lax.all_to_all(
-            normed_low, "grp", split_axis=1, concat_axis=0, tiled=True
-        ).reshape(2 * num_rows, half_width)
-        up_full, down_full, bias_full = gather_turned(
-            (w_up[layer_number, 0], down_weight[layer_number, 0], b_up[layer_number, 0]),
-            CH,
-            (1, 0, 0),
-        )
-        pre_act = product(group_rows, up_full) + bias_full.astype(jnp.float32)
-        grouped_output = product(exact_gelu(pre_act).astype(jnp.bfloat16), down_full)
+        group_rows = normed.astype(jnp.bfloat16).reshape(num_rows, 2, half_width)
+        up_full, down_full, bias_full = ffn_weights[layer_number]
+        pre_act = jnp.einsum(
+            "tgc,ghc->gth", group_rows, up_full, preferred_element_type=jnp.float32
+        ) + bias_full[:, None]
+        back_rows = jnp.einsum(
+            "gth,ghc->tgc",
+            exact_gelu(pre_act).astype(jnp.bfloat16),
+            down_full,
+            preferred_element_type=jnp.float32,
+        ).astype(jnp.bfloat16).reshape(num_rows, model_width)
         weights_kept = (up_full, down_full, pre_act)
-        back_rows = lax.all_to_all(
-            grouped_output.astype(jnp.bfloat16).reshape(2 * num_rows, 1, half_width),
-            "grp",
-            split_axis=0,
-            concat_axis=1,
-            tiled=True,
-        ).reshape(num_rows, model_width)
         resid_two = normed + back_rows.astype(jnp.float32) + b_down[layer_number]
         result = (
             norm_rows(resid_two, second_gain[layer_number], second_shift[layer_number]) * valid_rows
@@ -278,35 +568,27 @@
         )[1]
         d_resid_two, d_gain_two, d_shift_two = pull_two(grad_out * valid_rows)
         d_bdown = jnp.sum(d_resid_two, axis=0)
-        d_send = d_resid_two.astype(jnp.bfloat16).reshape(num_rows, 2, half_width)
-        d_group = lax.all_to_all(d_send, "grp", split_axis=1, concat_axis=0, tiled=True).reshape(
-            2 * num_rows, half_width
-        )
+        d_group = d_resid_two.astype(jnp.bfloat16).reshape(num_rows, 2, half_width)
         group_rows = kept["group_rows"]
         up_full, down_full, pre_act = kept["weights"]
         gelu_out, gelu_pull = jax.vjp(exact_gelu, pre_act)
-        d_pre = gelu_pull(product_t(d_group, down_full))[0].astype(jnp.bfloat16)
-        d_rows = product_t(d_pre, up_full)
-        d_up, d_down, d_upbias = (
-            summed_rows(inner_rows(group_rows, d_pre), (("ch_0", "ch_1", "ch_2"), "ch_3"), 1),
-            *side_by_side(
-                (inner_rows(gelu_out.astype(jnp.bfloat16), d_group), column_sum(d_pre)),
-                (("ch_0", "ch_1", "ch_2"), "ch_3"),
-                0,
-                1,
-            ),
-        )
+        d_pre = gelu_pull(
+            jnp.einsum("tgc,ghc->gth", d_group, down_full, preferred_element_type=jnp.float32)
+        )[0].astype(jnp.bfloat16)
         d_back = (
-            lax.all_to_all(
-                d_rows.reshape(2 * num_rows, 1, half_width).astype(jnp.bfloat16),
-                "grp",
-                split_axis=0,
-                concat_axis=1,
-                tiled=True,
-            )
+            jnp.einsum("gth,ghc->tgc", d_pre, up_full, preferred_element_type=jnp.float32)
+            .astype(jnp.bfloat16)
             .astype(jnp.float32)
             .reshape(num_rows, model_width)
         )
+        d_up = jnp.einsum("gth,tgc->ghc", d_pre, group_rows, preferred_element_type=jnp.float32)
+        d_down = jnp.einsum(
+            "gth,tgc->ghc",
+            gelu_out.astype(jnp.bfloat16),
+            d_group,
+            preferred_element_type=jnp.float32,
+        )
+        d_upbias = jnp.sum(d_pre.astype(jnp.float32), axis=1)
         pull_one = jax.vjp(
             norm_rows, kept["resid_one"], first_gain[layer_number], first_shift[layer_number]
         )[1]
@@ -421,9 +703,27 @@
             d_bdown,
             d_gain_two,
             d_shift_two,
-        )
-        return (d_input, layer_grads, (d_up, d_upbias, d_down))
-
+            d_upbias,
+        )
+        return (d_input, layer_grads, (d_up, d_down))
+
+    hidden_piece = w_up.shape[3]
+    pieces = jnp.concatenate([jnp.swapaxes(w_up[:, 0], 1, 2), down_weight[:, 0]], axis=1)
+    pieces = pieces.reshape(LAYERS, PARTS, 16, LANES).swapaxes(0, 1)
+    arrived = gather(pieces.reshape(PARTS, LAYERS * 16, LANES), LAYERS * 16, 1)
+    whole = jnp.stack([from_part(arrived[p], p) for p in range(PARTS)], axis=1)
+    whole = whole.reshape(2, 64, PARTS, LAYERS, 16, LANES)
+    whole = jnp.moveaxis(whole, 3, 0).reshape(LAYERS, 2, 64, 2, hidden_piece, LANES)
+    bias = lax.all_gather(b_up[:, 0], GRP_CH, axis=0).reshape(2, 64, LAYERS, hidden_piece)
+    bias = jnp.moveaxis(bias, 2, 0).reshape(LAYERS, 2, -1).astype(jnp.float32)
+    ffn_weights = [
+        (
+            whole[layer_pos, :, :, 0].reshape(2, -1, LANES),
+            whole[layer_pos, :, :, 1].reshape(2, -1, LANES),
+            bias[layer_pos],
+        )
+        for layer_pos in range(LAYERS)
+    ]
     current = start_x
     kept_all = []
     for layer_number in range(LAYERS):
@@ -447,20 +747,39 @@
                 ]
             )
         shared[layer_number] = layer_grads
-    stacked = tuple(
-        (
-            jnp.stack([shared[layer_pos][member] for layer_pos in range(LAYERS)])
-            for member in range(19)
-        )
-    )
-    totals = lax.psum(stacked + (seg_local,), GRP_CH)
-    grad_up = jnp.stack([sharded[layer_pos][0] for layer_pos in range(LAYERS)])[:, None]
-    grad_upbias = jnp.stack([sharded[layer_pos][1] for layer_pos in range(LAYERS)])[:, None]
-    grad_down = jnp.stack([sharded[layer_pos][2] for layer_pos in range(LAYERS)])[:, None]
+    members = [jnp.stack([shared[layer_pos][member] for layer_pos in range(LAYERS)]) for member in range(20)]
+    members.append(seg_local)
+    flat = [m.astype(jnp.bfloat16).reshape(-1) for m in members]
+    sizes = [f.shape[0] for f in flat]
+    total_rows = 128 * PARTS * 32
+    flat.append(jnp.zeros((total_rows * LANES - sum(sizes),), jnp.bfloat16))
+    small = jnp.concatenate(flat).reshape(PARTS, 2, 4, 4, 4, 32, LANES)
+    own = []
+    for layer_pos in range(LAYERS):
+        d_up, d_down = sharded[layer_pos]
+        rows = jnp.concatenate(
+            [d_up.reshape(128, hidden_piece, LANES), d_down.reshape(128, hidden_piece, LANES)], axis=1
+        ).astype(jnp.bfloat16)
+        own.append([to_part(rows[:, 16 * p : 16 * p + 16], p) for p in range(PARTS)])
+    both = jnp.concatenate([jnp.stack(own[0]), jnp.stack(own[1]), small], axis=-2)
+    summed, mine = exchange(both, 64, 32, 2)
+    summed = summed.reshape(-1).astype(jnp.float32)
+    totals, start = [], 0
+    for m, size in zip(members, sizes):
+        totals.append(summed[start : start + size].reshape(m.shape))
+        start += size
+    mine = mine[:, :32].astype(jnp.float32).reshape(PARTS, LAYERS, 16, LANES)
+    mine = jnp.moveaxis(mine, 1, 0).reshape(LAYERS, 2, hidden_piece, LANES)
+    grad_up = jnp.swapaxes(mine[:, 0], 1, 2)[:, None]
+    grad_down = mine[:, 1][:, None]
+    here_grp, here_ch = lax.axis_index("grp"), lax.axis_index(CH)
+    grad_upbias = lax.dynamic_slice(
+        totals[19], (0, here_grp, here_ch * hidden_piece), (LAYERS, 1, hidden_piece)
+    )
     return (
         current,
         grad_flow,
-        totals[19],
+        totals[20],
         totals[0],
         totals[1],
         totals[2],

time: 1090 us -> 965 us (0.89)
  waiting for transfers between devices: 444 us -> 0 us
  local copies, waits for them, and re-layouts: 187 us -> 366 us
  blocking collectives: 12.7 us -> 174 us
  Pallas kernels: 0 us -> 139 us
  starting transfers between devices: 68.8 us -> 0 us
  matrix products: 169 us -> 117 us
  other arithmetic: 178 us -> 146 us
  between operations: 18.4 us -> 5.49 us
    psum x2 -> x0, waiting for transfers between devices: 260 us -> none  [shards(): totals = lax.psum(stacked + (seg_local,), GRP_CH)]
    all_gather x0 -> x1, blocking collectives: none -> 174 us  [shards(): lax.all_gather(b_up[:, 0], GRP_CH, axis=0)]
    pallas_call x0 -> x2, Pallas kernels: none -> 139 us  [the longest x1 92.4 us: exchange(): pl.pallas_call(functools.partial(exchange_kernel, R, Rg), out_shape=(jax....]
    concatenate x2 -> x1, local copies, waits for them, and re-layouts: 1.2 us -> 139 us  [shards(): small = jnp.concatenate(flat).reshape(PARTS, 2, 4, 4, 4, 32, LANES)]
    all_gather x2 -> x0, waiting for transfers between devices: 119 us -> none  [gather_turned(): lax.all_gather(both, axis, axis=0, tiled=True)]
    all_to_all x14 -> x0, starting transfers between devices: 68.5 us -> none  [the longest x4 19.2 us: summed_rows(): lax.all_to_all(nearer, far, split_axis=0, concat_axis=0, tiled=True)]
    all_to_all x14 -> x0, waiting for transfers between devices: 64.9 us -> none  [the longest x4 48.8 us: summed_rows(): lax.all_to_all(nearer, far, split_axis=0, concat_axis=0, tiled=True)]
    dot_general x18 -> x14, matrix products: 51.9 us -> 11.5 us  [product(): return jnp.dot(first_op, second_op, preferred_element_type=jnp.float32)]
  transfers between devices with their start and end apart: 18 -> 0, of which waited for: 9 -> 0; matrix products, arithmetic and copies ran while one was open for 29% -> 0% of each run, Pallas kernels for 0% -> 0%
where the time goes in v1:
time: 965 us; the launch traced here: 947 us
  local copies, waits for them, and re-layouts  366 us (38%)
  blocking collectives  174 us (18%)
  other arithmetic  146 us (15%)
  Pallas kernels  139 us (14%)
  matrix products  117 us (12%)
    all_gather x1, blocking collectives, shards(): lax.all_gather(b_up[:, 0], GRP_CH, axis=0)  174 us
    concatenate x1, local copies, waits for them, and re-layouts, shards(): small = jnp.concatenate(flat).reshape(PARTS, 2, 4, 4, 4, 32, LANES)  139 us
    pallas_call x1, Pallas kernels, exchange(): pl.pallas_call(functools.partial(exchange_kernel, R, Rg), out_shape=(jax....  92.4 us
    pallas_call x1, Pallas kernels, gather(): pl.pallas_call(functools.partial(gather_kernel, R), out_shape=jax.ShapeDt...  46.1 us
    unnamed x673, local copies, waits for them, and re-layouts  39.6 us
    convert_element_type x2, other arithmetic, forward_layer(): exact_gelu(pre_act).astype(jnp.bfloat16)  31.8 us
    dot_general x14, matrix products, product_t(): lax.dot_general(first_op, second_op, (((1,), (1,)), ((), ())), preferred_...  29.5 us
    reshape x17, local copies, waits for them, and re-layouts, shards(): totals.append(summed[start:start + size].reshape(m.shape))  23.8 us

profile of v1, /device:TPU:1, one launch (start us, length us, event | category | flops | bytes accessed | tf_op | source)
XLA Modules:
  0.0 946.6 jit_solution(8789939197843404118)
XLA Ops:
  3.5 46.1 %shard_map.450 = bf16[3,2,4,4,4,32,384]{6,5,4,3,2,1,0:T(8,128)(2,1)} custom-call(bf16[3,32,384]{2,1,0:T(8,128)(2,1)} %bitcast.742), custom_call_target="tpu_custom_call" | custom-call | tf_op jit(solution)/shard_map/pallas_call | solution.py:332
  49.6 4.3 fusion.205
  55.7 4.7 maximum_bitcast_fusion
  60.4 8.3 copy.180
  68.6 6.9 fusion.204
  75.6 174.2 %all-gather = bf16[256,1,24]{2,1,0:T(2,128)(2,1)S(1)} all-gather(bf16[2,1,24]{2,1,0:T(2,128)(2,1)S(1)} %copy.182), channel_id=2, replica_groups=mesh['grp'=2,'ch_0'=4,'ch_1'=4,'ch_2'=2,'ch_3'=2] {'grp','ch_0','ch_1','..., dimensions={0}, use_global_device_ids=true | all-gather | bytes 12384 | tf_op jit(solution)/shard_map/all_gather | solution.py:717
  290.0 15.8 %multiply_convert_fusion.3 = (bf16[2,512,1536]{2,1,0:T(8,128)(2,1)S(1)}, f32[2,512,1536]{2,1,0:T(8,128)}) fusion(f32[2,512,1536]{2,1,0:T(8,128)S(1)} %get-tuple-element.426, f32[2,1536]{1,0:T(2,128)S(1)} %copy-done.212, u8[512,1536]{1,0:T(8,128)(4,1)S(1)} %get-tuple-element.184, u8[512,1536]{1,0:T(8,128)(4,1)S(1)} %get-tuple-element.183), kind=kLoop, calls=%fused_computation.37 | loop fusion | flops 111673344 | bytes 17313792 | tf_op jit(solution)/shard_map/convert_element_type | solution.py:539
  352.2 16.1 %multiply_convert_fusion.2 = (bf16[2,512,1536]{2,1,0:T(8,128)(2,1)S(1)}, f32[2,512,1536]{2,1,0:T(8,128)}) fusion(f32[2,512,1536]{2,1,0:T(8,128)S(1)} %get-tuple-element.432, f32[2,1536]{1,0:T(2,128)S(1)} %copy-done.214, u8[512,1536]{1,0:T(8,128)(4,1)S(1)} %get-tuple-element.182, u8[512,1536]{1,0:T(8,128)(4,1)S(1)} %get-tuple-element.181), kind=kLoop, calls=%fused_computation.21 | loop fusion | flops 111673344 | bytes 17313792 | tf_op jit(solution)/shard_map/convert_element_type | solution.py:539
  384.7 4.5 fusion.217
  406.6 4.6 multiply_reduce_fusion.23
  421.0 4.5 multiply_reduce_fusion.1
  447.1 4.6 multiply_reduce_fusion.3
  454.6 6.6 fusion.218
  475.8 4.1 multiply_reduce_fusion.14
  488.7 4.7 multiply_reduce_fusion
  594.9 139.3 %concatenate.51 = bf16[4718592]{0:T(1024)(128)(2,1)} concatenate(bf16[589824]{0:T(1024)(128)(2,1)S(1)} %convert_element_type.565, bf16[768]{0:T(1024)(128)(2,1)S(1)} %copy-done.273, bf16[589824]{0:T(1024)(128)(2,1)S(1)} %copy-done.31, bf16[589824]{0:T(1024)(128)(2,1)} %convert_element_type.570, bf16[768]{0:T(1024)(128)(2,1)S(1)} %copy-done.274, ...), dimensions={0} | concatenate | bytes 18874368 | tf_op jit(solution)/shard_map/concatenate | solution.py:756
  734.2 15.5 %reshape.1563 = bf16[3,2,4,4,4,32,384]{6,5,4,3,2,1,0:T(8,128)(2,1)} reshape(bf16[4718592]{0:T(1024)(128)(2,1)} %concatenate.51) | data formatting | bytes 18874368 | tf_op jit(solution)/shard_map/reshape | solution.py:756
  766.2 10.5 %pad_maximum_fusion.x = bf16[3,2,4,4,4,64,384]{6,5,4,3,2,1,0:T(8,128)(2,1)} fusion(bf16[3,2,4,4,4,32,384]{6,5,4,3,2,1,0:T(8,128)(2,1)S(1)} %bitcast.651, bf16[1,2,4,4,4,16,384]{6,5,4,3,2,1,0:T(8,128)(2,1)S(1)} %bitcast.663, bf16[1,2,4,4,4,16,384]{6,5,4,3,2,1,0:T(8,128)(2,1)S(1)} %bitcast.664, bf16[1,2,4,4,4,16,384]{6,5,4,3,2,1,0:T(8,128)(2,1)S(1)} %bitcast.665, ...), kind=kLoop, calls=%fused_computation | loop fusion | flops 132120576 | bytes 37748736 | tf_op jit(solution)/shard_map/concatenate | solution.py:764
  776.8 92.4 %shard_map.451 = (bf16[3,2,4,4,4,32,384]{6,5,4,3,2,1,0:T(8,128)(2,1)}, bf16[3,64,384]{2,1,0:T(8,128)(2,1)}) custom-call(bf16[3,2,4,4,4,64,384]{6,5,4,3,2,1,0:T(8,128)(2,1)} %pad_maximum_fusion.x), custom_call_target="tpu_custom_call" | custom-call | tf_op jit(solution)/shard_map/pallas_call | solution.py:309
  869.2 16.4 %reshape.1594 = f32[4718592]{0:T(1024)} reshape(bf16[3,2,4,4,4,32,384]{6,5,4,3,2,1,0:T(8,128)(2,1)} %get-tuple-element.119) | data formatting | bytes 28311552 | tf_op jit(solution)/shard_map/convert_element_type | solution.py:766
  889.9 13.0 %convert_element_type.608 = f32[3,2,4,4,4,32,384]{6,5,4,3,2,1,0:T(8,128)} convert(bf16[3,2,4,4,4,32,384]{6,5,4,3,2,1,0:T(8,128)(2,1)} %get-tuple-element.119) | non-fusion elementwise | flops 4718592 | bytes 28311552 | tf_op jit(solution)/shard_map/convert_element_type | solution.py:766
  904.2 7.5 fusion.202
  930.0 4.5 slice.867
  934.5 6.0 reshape.1573
  (1011 shorter events, 326.1 us)
Async XLA Ops:
  68.6 182.0 %copy-start.275 = (f32[2,768]{1,0:T(2,128)S(1)}, f32[2,768]{1,0:T(2,128)}, u32[]{:S(2)}) copy-start(f32[2,768]{1,0:T(2,128)} %param.45) | copy-start | bytes 18436
  68.6 182.0 %copy-start.276 = (f32[2,768]{1,0:T(2,128)S(1)}, f32[2,768]{1,0:T(2,128)}, u32[]{:S(2)}) copy-start(f32[2,768]{1,0:T(2,128)} %param.31) | copy-start | bytes 18436
  68.6 183.3 %copy-start.309 = (s32[128]{0:T(128)S(1)}, s32[128]{0:T(128)}, u32[]{:S(2)}) copy-start(s32[128]{0:T(128)} %param.29) | copy-start | bytes 1540
  68.6 184.6 %copy-start.310 = (s32[128]{0:T(128)S(1)}, s32[128]{0:T(128)}, u32[]{:S(2)}) copy-start(s32[128]{0:T(128)} %param.30) | copy-start | bytes 1540
  75.5 178.9 %copy-start.59 = (bf16[512,768]{1,0:T(8,128)(2,1)S(1)}, bf16[512,768]{1,0:T(8,128)(2,1)}, u32[]{:S(2)}) copy-start(bf16[512,768]{1,0:T(8,128)(2,1)} %param.27) | copy-start | bytes 2359300
  75.5 179.3 %copy-start.289 = (f32[2,384]{1,0:T(2,128)S(1)}, f32[2,384]{1,0:T(2,128)}, u32[]{:S(2)}) copy-start(f32[2,384]{1,0:T(2,128)} %param.43) | copy-start | bytes 9220
  253.2 23.6 %copy-start.201 = (pred[512]{0:T(512)(128)(4,1)}, pred[512]{0:T(512)(128)(4,1)S(1)}, u32[]{:S(2)}) copy-start(pred[512]{0:T(512)(128)(4,1)S(1)} %get-tuple-element.449) | copy-start | bytes 1540
  253.2 64.2 %copy-start.137 = (f32[512]{0:T(512)}, f32[512]{0:T(512)S(1)}, u32[]{:S(2)}) copy-start(f32[512]{0:T(512)S(1)} %get-tuple-element.450) | copy-start | bytes 6148
  254.8 17.7 %copy-start.10 = (bf16[512,768]{1,0:T(8,128)(2,1)}, bf16[512,768]{1,0:T(8,128)(2,1)S(1)}, u32[]{:S(2)}) copy-start(bf16[512,768]{1,0:T(8,128)(2,1)S(1)} %fusion.50) | copy-start | bytes 2359300
  271.3 10.0 %copy-start.120 = (bf16[1,512,6,64]{1,3,2,0:T(8,128)(2,1)}, bf16[1,512,6,64]{1,3,2,0:T(8,128)(2,1)S(1)}, u32[]{:S(2)}) copy-start(bf16[1,512,6,64]{1,3,2,0:T(8,128)(2,1)S(1)} %add_convert_fusion.9) | copy-start | bytes 1179652
  284.3 25.0 %copy-start.172 = (f32[768]{0:T(1024)}, f32[768]{0:T(1024)S(1)}, u32[]{:S(2)}) copy-start(f32[768]{0:T(1024)S(1)} %get-tuple-element.462) | copy-start | bytes 9220
  284.3 25.0 %copy-start.176 = (f32[512]{0:T(512)}, f32[512]{0:T(512)S(1)}, u32[]{:S(2)}) copy-start(f32[512]{0:T(512)S(1)} %broadcast_multiply_fusion.21) | copy-start | bytes 6148
  284.7 24.6 %copy-start.205 = (f32[512]{0:T(512)}, f32[512]{0:T(512)S(1)}, u32[]{:S(2)}) copy-start(f32[512]{0:T(512)S(1)} %fusion.170) | copy-start | bytes 6148
  290.0 15.8 %copy-start.25 = (f32[2,512,1536]{2,1,0:T(8,128)}, f32[2,512,1536]{2,1,0:T(8,128)S(1)}, u32[]{:S(2)}) copy-start(f32[2,512,1536]{2,1,0:T(8,128)S(1)} %get-tuple-element.426) | copy-start | bytes 18874372
  290.0 15.8 %copy-start.73 = (bf16[1,2,64,1,24,384]{5,4,3,2,1,0:T(8,128)(2,1)S(1)}, bf16[1,2,64,1,24,384]{5,4,3,2,1,0:T(8,128)(2,1)}, u32[]{:S(2)}) copy-start(bf16[1,2,64,1,24,384]{5,4,3,2,1,0:T(8,128)(2,1)} %get-tuple-element.330) | copy-start | bytes 7077892
  334.0 10.1 %copy-start.124 = (bf16[1,512,6,64]{1,3,2,0:T(8,128)(2,1)}, bf16[1,512,6,64]{1,3,2,0:T(8,128)(2,1)S(1)}, u32[]{:S(2)}) copy-start(bf16[1,512,6,64]{1,3,2,0:T(8,128)(2,1)S(1)} %add_convert_fusion.8) | copy-start | bytes 1179652
  352.2 16.1 %copy-start.26 = (f32[2,512,1536]{2,1,0:T(8,128)}, f32[2,512,1536]{2,1,0:T(8,128)S(1)}, u32[]{:S(2)}) copy-start(f32[2,512,1536]{2,1,0:T(8,128)S(1)} %get-tuple-element.432) | copy-start | bytes 18874372
  352.2 16.1 %copy-start.77 = (bf16[1,2,64,1,24,384]{5,4,3,2,1,0:T(8,128)(2,1)S(1)}, bf16[1,2,64,1,24,384]{5,4,3,2,1,0:T(8,128)(2,1)}, u32[]{:S(2)}) copy-start(bf16[1,2,64,1,24,384]{5,4,3,2,1,0:T(8,128)(2,1)} %get-tuple-element.329) | copy-start | bytes 7077892
  374.3 10.1 %copy-start.27 = (f32[2,512,1536]{2,1,0:T(8,128)S(1)}, f32[2,512,1536]{2,1,0:T(8,128)}, u32[]{:S(2)}) copy-start(f32[2,512,1536]{2,1,0:T(8,128)} %get-tuple-element.308) | copy-start | bytes 18874372
  535.5 28.1 %copy-start.57 = (bf16[1,512,768]{2,1,0:T(8,128)(2,1)S(1)}, bf16[1,512,768]{2,1,0:T(8,128)(2,1)}, u32[]{:S(2)}) copy-start(bf16[1,512,768]{2,1,0:T(8,128)(2,1)} %copy-done.56) | copy-start | bytes 2359300
  580.7 14.1 %copy-start.273 = (bf16[768]{0:T(1024)(128)(2,1)S(1)}, bf16[768]{0:T(1024)(128)(2,1)}, u32[]{:S(2)}) copy-start(bf16[768]{0:T(1024)(128)(2,1)} %convert_element_type.568) | copy-start | bytes 4612
  580.7 14.1 %copy-start.274 = (bf16[768]{0:T(1024)(128)(2,1)S(1)}, bf16[768]{0:T(1024)(128)(2,1)}, u32[]{:S(2)}) copy-start(bf16[768]{0:T(1024)(128)(2,1)} %convert_element_type.573) | copy-start | bytes 4612
  584.1 10.7 %copy-start.31 = (bf16[589824]{0:T(1024)(128)(2,1)S(1)}, bf16[589824]{0:T(1024)(128)(2,1)}, u32[]{:S(2)}) copy-start(bf16[589824]{0:T(1024)(128)(2,1)} %convert_element_type.569) | copy-start | bytes 3538948
  734.2 15.5 %copy-start.107 = (bf16[512,768]{1,0:T(8,128)(2,1)S(1)}, bf16[512,768]{1,0:T(8,128)(2,1)}, u32[]{:S(2)}) copy-start(bf16[512,768]{1,0:T(8,128)(2,1)} %copy-done.106) | copy-start | bytes 2359300
  (301 other events, 743.6 us)
